TPU v7x, 32 devices: a whole 2x2x4 slice. The times are simulated.
32 devices in a mesh: section: 4 (over z), ctx: 4 (over x, core), dp: 2 (over y).
Axes of the slice: x: 2, y: 2, z: 4, core: 2. Of those that a mesh axis runs over, the one named last changes fastest.
Arguments:
- stream: bfloat16 [4, 256, 8192], P('section', 'dp', 'ctx'), may hold values from -6 to 6
- norm_gain: float32 [4, 8192], P('section', 'ctx'), may hold values from 0.5 to 2
- w_router: bfloat16 [4, 8192], P('section', 'ctx'), may hold values from -0.0625 to 0.0625
- w_gate: bfloat16 [4, 8192, 14336], P('section', 'ctx', 'dp'), may hold values from -0.0625 to 0.0625
- w_up: bfloat16 [4, 8192, 14336], P('section', 'ctx', 'dp'), may hold values from -0.0625 to 0.0625
- w_down: bfloat16 [4, 14336, 8192], P('section', 'dp', 'ctx'), may hold values from -0.046875 to 0.046875
- keep_rows: int32 [2, 4, 2, 32], P(None, 'section', 'dp'), may hold values from -1 to 127, as said below
Outputs:
- advanced: bfloat16 [4, 256, 8192], P('section', 'dp', 'ctx')
Inputs may be any that keep to these rules, and one draw needn't show every extreme that they name: `keep_rows`: each list holds distinct row indices first, then -1 in its empty slots. Over the 2 lists of one tick and section exactly 32 rows are kept; in each tick and section some list is full and some is empty.
All inputs are finite; a program needn't handle non-finite values.
Results may differ from a plain program's by a relative error of at most 0.005.
Values may be sent and summed in bfloat16 or wider, within the bound.
A program may use at most 192 MiB of HBM per device.

v0:
```python
import jax
import jax.numpy as jnp
from jax import lax
from jax.sharding import PartitionSpec as P

D = 8192
eps = 1e-05


def from_behind(value, axis, steps):
    count = lax.axis_size(axis)
    pairs = [(source, (source + steps) % count) for source in range(count)]
    return lax.ppermute(value, axis, pairs)


def hidden_block(normed, w_gate, w_up, w_down):
    row_piece = lax.all_gather(normed, "dp", axis=0, tiled=True)
    gate_part = jnp.dot(row_piece, w_gate, preferred_element_type=jnp.float32)
    up_part = jnp.dot(row_piece, w_up, preferred_element_type=jnp.float32)
    partial_value = jnp.stack([gate_part, up_part], axis=1)
    summed = lax.psum(partial_value, "ctx")
    hidden = (jax.nn.silu(summed[:, 0]) * summed[:, 1]).astype(jnp.bfloat16)
    return lax.psum_scatter(
        jnp.dot(hidden, w_down, preferred_element_type=jnp.float32).astype(jnp.bfloat16),
        "dp",
        scatter_dimension=0,
        tiled=True,
    ).astype(jnp.float32)


def routed_layer(stream, keep_list, gain_row, router, w_gate, w_up, w_down):
    is_kept = keep_list >= 0
    picked = jnp.take(stream, jnp.maximum(keep_list, 0), axis=0)
    rows_wide = picked.astype(jnp.float32)
    squares = jnp.sum(rows_wide * rows_wide, axis=1)
    logits = jnp.sum(rows_wide * router.astype(jnp.float32)[None, :], axis=1)
    squares, logits = lax.psum((squares, logits), "ctx")
    scaling = lax.rsqrt(squares / D + eps)
    normed = jnp.where(
        is_kept[:, None], rows_wide * scaling[:, None] * gain_row[None, :], 0.0
    ).astype(jnp.bfloat16)
    update = hidden_block(normed, w_gate, w_up, w_down)
    new_rows = (rows_wide + jax.nn.sigmoid(logits)[:, None] * update).astype(jnp.bfloat16)
    target = jnp.where(is_kept, keep_list, stream.shape[0])
    return stream.at[target].set(new_rows, mode="drop")


def local(stream, norm_gain, w_router, w_gate, w_up, w_down, keep_rows):
    first_pass = routed_layer(
        stream[0], keep_rows[0, 0, 0], norm_gain[0], w_router[0], w_gate[0], w_up[0], w_down[0]
    )
    passed = from_behind(first_pass, "section", 1)
    second_pass = routed_layer(
        passed, keep_rows[1, 0, 0], norm_gain[0], w_router[0], w_gate[0], w_up[0], w_down[0]
    )
    section_place = lax.axis_index("section")
    result = jnp.where(section_place == 0, passed, second_pass)
    return result[None]


def solution(mesh):
    return jax.shard_map(
        local,
        mesh=mesh,
        in_specs=(
            P("section", "dp", "ctx"),
            P("section", "ctx"),
            P("section", "ctx"),
            P("section", "ctx", "dp"),
            P("section", "ctx", "dp"),
            P("section", "dp", "ctx"),
            P(None, "section", "dp", None),
        ),
        out_specs=P("section", "dp", "ctx"),
        check_vma=False,
    )
```

profile of v0, /device:TPU:0, one launch (start us, length us, event | category | flops | bytes accessed | tf_op | source)
XLA Modules:
  0.0 325.9 jit_solution(13672440571319732338)
XLA Ops:
  6.5 1.0 copy.13
  8.9 0.7 mul.113
  10.5 8.3 %all-reduce.1 = (f32[32]{0:T(128)S(1)}, f32[32]{0:T(128)S(1)}) all-reduce(f32[32]{0:T(128)S(1)} %get-tuple-element.9, f32[32]{0:T(128)S(1)} %get-tuple-element.8), channel_id=1, replica_groups=mesh['section'=4,'ctx'=4,'dp'=2] {'ctx'}, use_global_device_ids=true, to_apply=%region_3.5 | all-reduce | flops 64 | bytes 512 | tf_op jit(solution)/shard_map/psum | solution.py:37
  18.9 0.8 fusion.40
  19.7 5.6 %all_gather.6 = bf16[64,2048]{1,0:T(8,128)(2,1)S(1)} all-gather(bf16[32,2048]{1,0:T(8,128)(2,1)S(1)} %fusion.40), channel_id=1, replica_groups=mesh['section'=4,'ctx'=4,'dp'=2] {'dp'}, dimensions={0}, use_global_device_ids=true | all-gather | bytes 393216 | tf_op jit(solution)/shard_map/all_gather | solution.py:17
  25.4 12.0 %fusion.12 = f32[64,1,7168]{2,0,1:T(8,128)S(1)} fusion(bf16[64,2048]{1,0:T(8,128)(2,1)S(1)} %all_gather.6, bf16[1,2048,7168]{2,1,0:T(8,128)(2,1)} %param.12), kind=kOutput, calls=%fused_computation.16 | convolution fusion | flops 1879048192 | bytes 31457280 | tf_op jit(solution)/shard_map/dot_general | solution.py:18
  37.3 12.0 %fusion.18 = f32[64,1,7168]{2,0,1:T(8,128)S(1)} fusion(bf16[64,2048]{1,0:T(8,128)(2,1)S(1)} %all_gather.6, bf16[1,2048,7168]{2,1,0:T(8,128)(2,1)} %param.13), kind=kOutput, calls=%fused_computation.18 | convolution fusion | flops 1879048192 | bytes 31457280 | tf_op jit(solution)/shard_map/dot_general | solution.py:19
  49.3 2.1 pad_maximum_fusion
  51.5 77.4 %all-reduce.5.cloned.1.call-done = f32[64,2,7168]{2,0,1:T(8,128)} async-done(((f32[64,2,7168]{2,0,1:T(8,128)}), f32[64,2,7168]{2,0,1:T(8,128)}) %all-reduce.5.cloned.1.call-update) | async-done | bytes 3670032 | tf_op jit(solution)/shard_map/psum | solution.py:21
  128.9 16.4 %fusion.24 = bf16[64,2048]{1,0:T(8,128)(2,1)} fusion(bf16[1,7168,2048]{2,1,0:T(8,128)(2,1)} %param.14, f32[64,2,7168]{2,0,1:T(8,128)} %all-reduce.5.cloned.1.call-done), kind=kOutput, calls=%fused_computation.22 | convolution fusion | flops 1881931776 | bytes 33292288 | tf_op jit(solution)/shard_map/dot_general | solution.py:24
  145.4 11.9 %reduce-scatter.3.cloned.1.call-done = bf16[32,2048]{1,0:T(8,128)(2,1)} async-done(((bf16[64,2048]{1,0:T(8,128)(2,1)}), bf16[32,2048]{1,0:T(8,128)(2,1)}) %reduce-scatter.3.cloned.1.call-update) | async-done | bytes 131088 | tf_op jit(solution)/shard_map/reduce_scatter | solution.py:23
  157.3 1.6 scatter_custom_fusion
  158.9 1.5 collective-permute-start
  160.4 14.0 %collective-permute-done = bf16[128,2048]{1,0:T(8,128)(2,1)S(1)} collective-permute-done((bf16[128,2048]{1,0:T(8,128)(2,1)S(1)}, bf16[128,2048]{1,0:T(8,128)(2,1)S(1)}, u32[]{:S(2)}, u32[]{:S(2)}) %collective-permute-start) | collective-permute-done | bytes 524320 | tf_op jit(solution)/shard_map/ppermute | solution.py:13
  175.3 5.7 %all-reduce = (f32[32]{0:T(128)S(1)}, f32[32]{0:T(128)S(1)}) all-reduce(f32[32]{0:T(128)S(1)} %get-tuple-element.7, f32[32]{0:T(128)S(1)} %get-tuple-element.6), channel_id=1, replica_groups=mesh['section'=4,'ctx'=4,'dp'=2] {'ctx'}, use_global_device_ids=true, to_apply=%region_10.12 | all-reduce | flops 64 | bytes 512 | tf_op jit(solution)/shard_map/psum | solution.py:37
  181.1 6.1 %all_gather.7 = bf16[64,2048]{1,0:T(8,128)(2,1)S(1)} all-gather(bf16[32,2048]{1,0:T(8,128)(2,1)S(1)} %fusion.46), channel_id=1, replica_groups=mesh['section'=4,'ctx'=4,'dp'=2] {'dp'}, dimensions={0}, use_global_device_ids=true | all-gather | bytes 393216 | tf_op jit(solution)/shard_map/all_gather | solution.py:17
  187.2 12.0 %fusion.15 = f32[64,1,7168]{2,0,1:T(8,128)S(1)} fusion(bf16[64,2048]{1,0:T(8,128)(2,1)S(1)} %all_gather.7, bf16[1,2048,7168]{2,1,0:T(8,128)(2,1)} %param.12), kind=kOutput, calls=%fused_computation.17 | convolution fusion | flops 1879048192 | bytes 31457280 | tf_op jit(solution)/shard_map/dot_general | solution.py:18
  199.2 12.0 %fusion.21 = f32[64,1,7168]{2,0,1:T(8,128)S(1)} fusion(bf16[64,2048]{1,0:T(8,128)(2,1)S(1)} %all_gather.7, bf16[1,2048,7168]{2,1,0:T(8,128)(2,1)} %param.13), kind=kOutput, calls=%fused_computation.19 | convolution fusion | flops 1879048192 | bytes 31457280 | tf_op jit(solution)/shard_map/dot_general | solution.py:19
  211.2 2.1 pad_maximum_fusion.1
  213.4 75.2 %all-reduce.7.cloned.1.call-done = f32[64,2,7168]{2,0,1:T(8,128)} async-done(((f32[64,2,7168]{2,0,1:T(8,128)}), f32[64,2,7168]{2,0,1:T(8,128)}) %all-reduce.7.cloned.1.call-update) | async-done | bytes 3670032 | tf_op jit(solution)/shard_map/psum | solution.py:21
  288.6 16.4 %fusion.27 = bf16[64,2048]{1,0:T(8,128)(2,1)} fusion(bf16[1,7168,2048]{2,1,0:T(8,128)(2,1)} %param.14, f32[64,2,7168]{2,0,1:T(8,128)} %all-reduce.7.cloned.1.call-done), kind=kOutput, calls=%fused_computation.23 | convolution fusion | flops 1881931776 | bytes 33292288 | tf_op jit(solution)/shard_map/dot_general | solution.py:24
  305.1 11.9 %reduce-scatter.5.cloned.1.call-done = bf16[32,2048]{1,0:T(8,128)(2,1)} async-done(((bf16[64,2048]{1,0:T(8,128)(2,1)}), bf16[32,2048]{1,0:T(8,128)(2,1)}) %reduce-scatter.5.cloned.1.call-update) | async-done | bytes 131088 | tf_op jit(solution)/shard_map/reduce_scatter | solution.py:23
  316.9 1.6 scatter_custom_fusion.1
  318.5 0.9 select_bitcast_fusion
  (27 shorter events, 3.5 us)
Async XLA Ops:
  6.5 122.4 %all-reduce.5.cloned.1.call-start = ((), (), s32[]{:S(2)}) async-start(), calls=%async_computation.2 | async-start | bytes 7340032 | tf_op jit(solution)/shard_map/psum | solution.py:21
  51.5 93.9 %copy-start.1 = (s32[2,1,1,32]{3,2,1,0:T(1,128)S(1)}, s32[2,1,1,32]{3,2,1,0:T(1,128)}, u32[]{:S(2)}) copy-start(s32[2,1,1,32]{3,2,1,0:T(1,128)} %param.15) | copy-start | bytes 772
  51.5 129.5 %copy-start = (f32[1,2048]{1,0:T(1,128)S(1)}, f32[1,2048]{1,0:T(1,128)}, u32[]{:S(2)}) copy-start(f32[1,2048]{1,0:T(1,128)} %param.10) | copy-start | bytes 24580
  51.5 105.8 %reduce-scatter.3.cloned.1.call-start = ((), (), s32[]{:S(2)}) async-start(), calls=%async_computation.3 | async-start | bytes 393216 | tf_op jit(solution)/shard_map/reduce_scatter | solution.py:23
  145.3 143.3 %all-reduce.7.cloned.1.call-start = ((), (), s32[]{:S(2)}) async-start(), calls=%async_computation.4 | async-start | bytes 7340032 | tf_op jit(solution)/shard_map/psum | solution.py:21
  158.9 15.5 %collective-permute-start = (bf16[128,2048]{1,0:T(8,128)(2,1)S(1)}, bf16[128,2048]{1,0:T(8,128)(2,1)S(1)}, u32[]{:S(2)}, u32[]{:S(2)}) collective-permute-start(bf16[128,2048]{1,0:T(8,128)(2,1)S(1)} %scatter_custom_fusion), channel_id=1, source_target_pairs={{0,8},{8,16},{16,24},{24,0},{1,9},{9,17},{17,25},{25,1},{2,10},{10... | collective-permute-start | bytes 1572872 | tf_op jit(solution)/shard_map/ppermute | solution.py:13
  213.3 103.6 %reduce-scatter.5.cloned.1.call-start = ((), (), s32[]{:S(2)}) async-start(), calls=%async_computation.5 | async-start | bytes 393216 | tf_op jit(solution)/shard_map/reduce_scatter | solution.py:23
Sparse Core Ops, SparseCore 0:
  51.6 77.3 all-reduce.4
  145.5 11.7 reduce-scatter.2
  213.4 75.1 all-reduce.6
  305.1 11.7 reduce-scatter.4
where the time goes:
time: 326 us
  waiting for transfers between devices  190 us (58%)
  matrix products  80.7 us (25%)
  blocking collectives  25.8 us (8%)
  between operations  13.3 us (4%)
  other arithmetic  11.7 us (4%)
    psum x2, waiting for transfers between devices, hidden_block(): summed = lax.psum(partial_value, 'ctx')  153 us
    dot_general x2, matrix products, hidden_block(): jnp.dot(hidden, w_down, preferred_element_type=jnp.float32)  32.8 us
    dot_general x2, matrix products, hidden_block(): up_part = jnp.dot(row_piece, w_up, preferred_element_type=jnp.float32)  24 us
    dot_general x2, matrix products, hidden_block(): gate_part = jnp.dot(row_piece, w_gate, preferred_element_type=jnp.float32)  24 us
    reduce_scatter x2, waiting for transfers between devices, hidden_block(): lax.psum_scatter(jnp.dot(hidden, w_down, preferred_element_type=jnp.float...  23.7 us
    psum x2, blocking collectives, routed_layer(): squares, logits = lax.psum((squares, logits), 'ctx')  14 us
    ppermute x1, waiting for transfers between devices, from_behind(): return lax.ppermute(value, axis, pairs)  14 us
    all_gather x2, blocking collectives, hidden_block(): row_piece = lax.all_gather(normed, 'dp', axis=0, tiled=True)  11.7 us
  transfers between devices with their start and end apart: 5, of which 5 were waited for; matrix products, arithmetic and copies ran while one was open for 0% of the time, Pallas kernels for 0%

commit v1 on v0

--- a/solution.py
+++ b/solution.py
@@ -18,7 +18,10 @@
     gate_part = jnp.dot(row_piece, w_gate, preferred_element_type=jnp.float32)
     up_part = jnp.dot(row_piece, w_up, preferred_element_type=jnp.float32)
     partial_value = jnp.stack([gate_part, up_part], axis=1)
-    summed = lax.psum(partial_value, "ctx")
+    size, summed = (lax.axis_size("ctx"), partial_value)
+    for stride in [1 << k for k in range(size.bit_length() - 1)]:
+        swap = [(i, i ^ stride) for i in range(size)]
+        summed = summed + lax.ppermute(summed, "ctx", swap)
     hidden = (jax.nn.silu(summed[:, 0]) * summed[:, 1]).astype(jnp.bfloat16)
     return lax.psum_scatter(
         jnp.dot(hidden, w_down, preferred_element_type=jnp.float32).astype(jnp.bfloat16),

time: 326 us -> 340 us (1.043)
  waiting for transfers between devices: 190 us -> 210 us
  matrix products: 80.7 us -> 73.6 us
    ppermute x0 -> x4, waiting for transfers between devices: none -> 173 us  [hidden_block(): summed = summed + lax.ppermute(summed, 'ctx', swap)]
    psum x2 -> x0, waiting for transfers between devices: 153 us -> none  [hidden_block(): summed = lax.psum(partial_value, 'ctx')]
    dot_general x2, matrix products: 32.8 us -> 25.6 us  [hidden_block(): jnp.dot(hidden, w_down, preferred_element_type=jnp.float32)]
    another operation x2, other arithmetic: 4.17 us -> 0.5 us  [hidden_block(): partial_value = jnp.stack([gate_part, up_part], axis=1)]
  transfers between devices with their start and end apart: 5 -> 7, of which waited for: 5 -> 7; matrix products, arithmetic and copies ran while one was open for 0% -> 0% of each run, Pallas kernels for 0% -> 0%
where the time goes in v1:
time: 340 us; the launch traced here: 339 us
  waiting for transfers between devices  210 us (62%)
  matrix products  73.6 us (22%)
  blocking collectives  25.8 us (8%)
  between operations  13.6 us (4%)
  other arithmetic  10.4 us (3%)
  starting transfers between devices  3.92 us (1%)
    ppermute x4, waiting for transfers between devices, hidden_block(): summed = summed + lax.ppermute(summed, 'ctx', swap)  173 us
    dot_general x2, matrix products, hidden_block(): jnp.dot(hidden, w_down, preferred_element_type=jnp.float32)  25.6 us
    dot_general x2, matrix products, hidden_block(): up_part = jnp.dot(row_piece, w_up, preferred_element_type=jnp.float32)  24 us
    dot_general x2, matrix products, hidden_block(): gate_part = jnp.dot(row_piece, w_gate, preferred_element_type=jnp.float32)  24 us
    reduce_scatter x2, waiting for transfers between devices, hidden_block(): lax.psum_scatter(jnp.dot(hidden, w_down, preferred_element_type=jnp.float...  22 us
    psum x2, blocking collectives, routed_layer(): squares, logits = lax.psum((squares, logits), 'ctx')  14 us
    ppermute x1, waiting for transfers between devices, from_behind(): return lax.ppermute(value, axis, pairs)  14 us
    all_gather x2, blocking collectives, hidden_block(): row_piece = lax.all_gather(normed, 'dp', axis=0, tiled=True)  11.7 us
  transfers between devices with their start and end apart: 7, of which 7 were waited for; matrix products, arithmetic and copies ran while one was open for 0% of the time, Pallas kernels for 0%

profile of v1, /device:TPU:0, one launch (start us, length us, event | category | flops | bytes accessed | tf_op | source)
XLA Modules:
  0.0 339.2 jit_solution(2210092652899768007)
XLA Ops:
  6.5 1.0 copy.11
  10.5 8.3 %all-reduce.1 = (f32[32]{0:T(128)S(1)}, f32[32]{0:T(128)S(1)}) all-reduce(f32[32]{0:T(128)S(1)} %get-tuple-element.9, f32[32]{0:T(128)S(1)} %get-tuple-element.8), channel_id=1, replica_groups=mesh['section'=4,'ctx'=4,'dp'=2] {'ctx'}, use_global_device_ids=true, to_apply=%region_3.5 | all-reduce | flops 64 | bytes 512 | tf_op jit(solution)/shard_map/psum | solution.py:40
  18.9 0.8 fusion.40
  19.7 5.6 %all_gather.6 = bf16[64,2048]{1,0:T(8,128)(2,1)S(1)} all-gather(bf16[32,2048]{1,0:T(8,128)(2,1)S(1)} %fusion.40), channel_id=1, replica_groups=mesh['section'=4,'ctx'=4,'dp'=2] {'dp'}, dimensions={0}, use_global_device_ids=true | all-gather | bytes 393216 | tf_op jit(solution)/shard_map/all_gather | solution.py:17
  25.4 12.0 %fusion.12 = f32[64,1,7168]{2,0,1:T(8,128)S(1)} fusion(bf16[64,2048]{1,0:T(8,128)(2,1)S(1)} %all_gather.6, bf16[1,2048,7168]{2,1,0:T(8,128)(2,1)} %param.12), kind=kOutput, calls=%fused_computation.16 | convolution fusion | flops 1879048192 | bytes 31457280 | tf_op jit(solution)/shard_map/dot_general | solution.py:18
  37.3 12.0 %fusion.18 = f32[64,1,7168]{2,0,1:T(8,128)S(1)} fusion(bf16[64,2048]{1,0:T(8,128)(2,1)S(1)} %all_gather.6, bf16[1,2048,7168]{2,1,0:T(8,128)(2,1)} %param.13), kind=kOutput, calls=%fused_computation.18 | convolution fusion | flops 1879048192 | bytes 31457280 | tf_op jit(solution)/shard_map/dot_general | solution.py:19
  49.7 6.4 %collective-permute-done = f32[64,2,7168]{2,0,1:T(8,128)S(1)} collective-permute-done((f32[64,2,7168]{2,0,1:T(8,128)S(1)}, f32[64,2,7168]{2,0,1:T(8,128)S(1)}, u32[]{:S(2)}, u32[]{:S(2)}) %collective-permute-start) | collective-permute-done | bytes 3670048 | tf_op jit(solution)/shard_map/ppermute | solution.py:24
  57.3 80.8 %collective-permute-done.1 = f32[64,2,7168]{2,0,1:T(8,128)S(1)} collective-permute-done((f32[64,2,7168]{2,0,1:T(8,128)S(1)}, f32[64,2,7168]{2,0,1:T(8,128)S(1)}, u32[]{:S(2)}, u32[]{:S(2)}) %collective-permute-start.1) | collective-permute-done | bytes 3670048 | tf_op jit(solution)/shard_map/ppermute | solution.py:24
  138.8 12.8 %fusion.24 = bf16[64,2048]{1,0:T(8,128)(2,1)} fusion(bf16[1,7168,2048]{2,1,0:T(8,128)(2,1)} %param.14, f32[64,2,7168]{2,0,1:T(8,128)S(1)} %fusion.65), kind=kOutput, calls=%fused_computation.22 | convolution fusion | flops 1881931776 | bytes 33292288 | tf_op jit(solution)/shard_map/dot_general | solution.py:27
  151.7 12.1 %reduce-scatter.3.cloned.1.call-done = bf16[32,2048]{1,0:T(8,128)(2,1)} async-done(((bf16[64,2048]{1,0:T(8,128)(2,1)}), bf16[32,2048]{1,0:T(8,128)(2,1)}) %reduce-scatter.3.cloned.1.call-update) | async-done | bytes 131088 | tf_op jit(solution)/shard_map/reduce_scatter | solution.py:26
  163.8 1.6 scatter_custom_fusion
  165.3 1.5 collective-permute-start.2
  166.9 14.0 %collective-permute-done.2 = bf16[128,2048]{1,0:T(8,128)(2,1)S(1)} collective-permute-done((bf16[128,2048]{1,0:T(8,128)(2,1)S(1)}, bf16[128,2048]{1,0:T(8,128)(2,1)S(1)}, u32[]{:S(2)}, u32[]{:S(2)}) %collective-permute-start.2) | collective-permute-done | bytes 524320 | tf_op jit(solution)/shard_map/ppermute | solution.py:13
  181.7 5.7 %all-reduce = (f32[32]{0:T(128)S(1)}, f32[32]{0:T(128)S(1)}) all-reduce(f32[32]{0:T(128)S(1)} %get-tuple-element.7, f32[32]{0:T(128)S(1)} %get-tuple-element.6), channel_id=1, replica_groups=mesh['section'=4,'ctx'=4,'dp'=2] {'ctx'}, use_global_device_ids=true, to_apply=%region_9.11 | all-reduce | flops 64 | bytes 512 | tf_op jit(solution)/shard_map/psum | solution.py:40
  187.6 6.1 %all_gather.7 = bf16[64,2048]{1,0:T(8,128)(2,1)S(1)} all-gather(bf16[32,2048]{1,0:T(8,128)(2,1)S(1)} %fusion.46), channel_id=1, replica_groups=mesh['section'=4,'ctx'=4,'dp'=2] {'dp'}, dimensions={0}, use_global_device_ids=true | all-gather | bytes 393216 | tf_op jit(solution)/shard_map/all_gather | solution.py:17
  193.7 12.0 %fusion.15 = f32[64,1,7168]{2,0,1:T(8,128)S(1)} fusion(bf16[64,2048]{1,0:T(8,128)(2,1)S(1)} %all_gather.7, bf16[1,2048,7168]{2,1,0:T(8,128)(2,1)} %param.12), kind=kOutput, calls=%fused_computation.17 | convolution fusion | flops 1879048192 | bytes 31457280 | tf_op jit(solution)/shard_map/dot_general | solution.py:18
  205.7 12.0 %fusion.21 = f32[64,1,7168]{2,0,1:T(8,128)S(1)} fusion(bf16[64,2048]{1,0:T(8,128)(2,1)S(1)} %all_gather.7, bf16[1,2048,7168]{2,1,0:T(8,128)(2,1)} %param.13), kind=kOutput, calls=%fused_computation.19 | convolution fusion | flops 1879048192 | bytes 31457280 | tf_op jit(solution)/shard_map/dot_general | solution.py:19
  218.0 6.4 %collective-permute-done.3 = f32[64,2,7168]{2,0,1:T(8,128)S(1)} collective-permute-done((f32[64,2,7168]{2,0,1:T(8,128)S(1)}, f32[64,2,7168]{2,0,1:T(8,128)S(1)}, u32[]{:S(2)}, u32[]{:S(2)}) %collective-permute-start.3) | collective-permute-done | bytes 3670048 | tf_op jit(solution)/shard_map/ppermute | solution.py:24
  224.9 1.5 collective-permute-start.4
  226.4 79.9 %collective-permute-done.4 = f32[64,2,7168]{2,0,1:T(8,128)S(1)} collective-permute-done((f32[64,2,7168]{2,0,1:T(8,128)S(1)}, f32[64,2,7168]{2,0,1:T(8,128)S(1)}, u32[]{:S(2)}, u32[]{:S(2)}) %collective-permute-start.4) | collective-permute-done | bytes 3670048 | tf_op jit(solution)/shard_map/ppermute | solution.py:24
  307.1 12.8 %fusion.27 = bf16[64,2048]{1,0:T(8,128)(2,1)} fusion(bf16[1,7168,2048]{2,1,0:T(8,128)(2,1)} %param.14, f32[64,2,7168]{2,0,1:T(8,128)S(1)} %fusion.64), kind=kOutput, calls=%fused_computation.23 | convolution fusion | flops 1881931776 | bytes 33292288 | tf_op jit(solution)/shard_map/dot_general | solution.py:27
  320.0 9.9 %reduce-scatter.5.cloned.1.call-done = bf16[32,2048]{1,0:T(8,128)(2,1)} async-done(((bf16[64,2048]{1,0:T(8,128)(2,1)}), bf16[32,2048]{1,0:T(8,128)(2,1)}) %reduce-scatter.5.cloned.1.call-update) | async-done | bytes 131088 | tf_op jit(solution)/shard_map/reduce_scatter | solution.py:26
  329.9 1.6 scatter_custom_fusion.1
  331.5 0.9 select_bitcast_fusion
  (33 shorter events, 7.8 us)
Async XLA Ops:
  6.5 157.2 %reduce-scatter.3.cloned.1.call-start = ((), (), s32[]{:S(2)}) async-start(), calls=%async_computation.2 | async-start | bytes 393216 | tf_op jit(solution)/shard_map/reduce_scatter | solution.py:26
  49.6 6.5 %collective-permute-start = (f32[64,2,7168]{2,0,1:T(8,128)S(1)}, f32[64,2,7168]{2,0,1:T(8,128)S(1)}, u32[]{:S(2)}, u32[]{:S(2)}) collective-permute-start(f32[64,2,7168]{2,0,1:T(8,128)S(1)} %pad_maximum_fusion), channel_id=1, source_target_pairs={{0,2},{2,0},{4,6},{6,4},{1,3},{3,1},{5,7},{7,5},{8,10},{10,8},{12,... | collective-permute-start | bytes 11010056 | tf_op jit(solution)/shard_map/ppermute | solution.py:24
  56.6 81.4 %collective-permute-start.1 = (f32[64,2,7168]{2,0,1:T(8,128)S(1)}, f32[64,2,7168]{2,0,1:T(8,128)S(1)}, u32[]{:S(2)}, u32[]{:S(2)}) collective-permute-start(f32[64,2,7168]{2,0,1:T(8,128)S(1)} %fusion.59), channel_id=1, source_target_pairs={{0,4},{2,6},{4,0},{6,2},{1,5},{3,7},{5,1},{7,3},{8,12},{10,14},{12... | collective-permute-start | bytes 11010056 | tf_op jit(solution)/shard_map/ppermute | solution.py:24
  138.7 12.9 %copy-start.1 = (s32[2,1,1,32]{3,2,1,0:T(1,128)S(1)}, s32[2,1,1,32]{3,2,1,0:T(1,128)}, u32[]{:S(2)}) copy-start(s32[2,1,1,32]{3,2,1,0:T(1,128)} %param.15) | copy-start | bytes 772
  138.7 48.7 %copy-start = (f32[1,2048]{1,0:T(1,128)S(1)}, f32[1,2048]{1,0:T(1,128)}, u32[]{:S(2)}) copy-start(f32[1,2048]{1,0:T(1,128)} %param.10) | copy-start | bytes 24580
  151.6 178.3 %reduce-scatter.5.cloned.1.call-start = ((), (), s32[]{:S(2)}) async-start(), calls=%async_computation.3 | async-start | bytes 393216 | tf_op jit(solution)/shard_map/reduce_scatter | solution.py:26
  165.3 15.5 %collective-permute-start.2 = (bf16[128,2048]{1,0:T(8,128)(2,1)S(1)}, bf16[128,2048]{1,0:T(8,128)(2,1)S(1)}, u32[]{:S(2)}, u32[]{:S(2)}) collective-permute-start(bf16[128,2048]{1,0:T(8,128)(2,1)S(1)} %scatter_custom_fusion), channel_id=1, source_target_pairs={{0,8},{8,16},{16,24},{24,0},{1,9},{9,17},{17,25},{25,1},{2,10},{10... | collective-permute-start | bytes 1572872 | tf_op jit(solution)/shard_map/ppermute | solution.py:13
  217.9 6.5 %collective-permute-start.3 = (f32[64,2,7168]{2,0,1:T(8,128)S(1)}, f32[64,2,7168]{2,0,1:T(8,128)S(1)}, u32[]{:S(2)}, u32[]{:S(2)}) collective-permute-start(f32[64,2,7168]{2,0,1:T(8,128)S(1)} %pad_maximum_fusion.1), channel_id=1, source_target_pairs={{0,2},{2,0},{4,6},{6,4},{1,3},{3,1},{5,7},{7,5},{8,10},{10,8},{12,... | collective-permute-start | bytes 11010056 | tf_op jit(solution)/shard_map/ppermute | solution.py:24
  224.9 81.4 %collective-permute-start.4 = (f32[64,2,7168]{2,0,1:T(8,128)S(1)}, f32[64,2,7168]{2,0,1:T(8,128)S(1)}, u32[]{:S(2)}, u32[]{:S(2)}) collective-permute-start(f32[64,2,7168]{2,0,1:T(8,128)S(1)} %fusion.58), channel_id=1, source_target_pairs={{0,4},{2,6},{4,0},{6,2},{1,5},{3,7},{5,1},{7,3},{8,12},{10,14},{12... | collective-permute-start | bytes 11010056 | tf_op jit(solution)/shard_map/ppermute | solution.py:24
Sparse Core Ops, SparseCore 0:
  151.7 12.0 reduce-scatter.2
  320.0 9.8 reduce-scatter.4
